TPU v7x, 512 devices: a whole 4x4x16 slice. The times are simulated.
512 devices in a mesh: dp: 128 (over z, y, core), mp: 4 (over x).
Axes of the slice: x: 4, y: 4, z: 16, core: 2. Of those that a mesh axis runs over, the one named last changes fastest.
Arguments:
- hidden_in: bfloat16 [65536, 4096], P('dp', 'mp'), as said below
- grad_out: bfloat16 [65536, 4096], P('dp', 'mp'), may hold values from -3 to 3
- grad_qkv: bfloat16 [32768, 6144], P('dp', 'mp'), may hold values from -6 to 6
- qkv_weight: bfloat16 [4096, 6144], P('dp', 'mp'), may hold values from -0.09375 to 0.09375
- norm_gain: float32 [4096], P('mp'), may hold values from 0.1 to 1.9
- image_count: int32 [128], P('dp'), may hold values from 0 to 512, as said below
- image_pos: int32 [65536], P('dp'), may hold values from 0 to 512, as said below
- block_slot: int32 [128, 4], P('dp'), may hold values from -1 to 7, as said below
Outputs:
- grad_in: bfloat16 [65536, 4096], P('dp', 'mp')
Inputs may be any that keep to these rules, and one draw needn't show every extreme that they name: `image_count`: each shard's count of image tokens; it is at most 512. `image_pos`: for shard i, its first image_count[i] entries are distinct increasing positions below 512; the remaining entries equal 512. `block_slot`: entry b of shard i is -1 exactly when b * 128 >= image_count[i]. Otherwise v // 2 < 4 and the block's cotangent lies in work slot v mod 2 of data index (i + v // 2) mod 128. No work slot is named twice; some data index has all 2 of its work slots named. Work slots that no block names hold rows of no token. `hidden_in`: activations of a real residual stream.
All inputs are finite; a program needn't handle non-finite values.
Results may differ from a plain program's by a relative error of at most 0.0095.
Values may be sent and summed in bfloat16 or wider, within the bound.
A program may use at most 64 MiB of HBM per device.

v0:
```python
import jax
import jax.numpy as jnp
from jax import lax
from jax.sharding import PartitionSpec as P

D = 4096
BLK = 4
REACH = 4
WORKB = 2


def from_behind(block, axis, distance):
    devices = range(lax.axis_size(axis))
    route = [((i - distance) % len(devices), i) for i in devices]
    return lax.ppermute(block, axis, route)


def shards(
    hidden_in, grad_out, grad_qkv, qkv_weight, norm_gain, image_count, image_pos, block_slot
):
    seq_rows = hidden_in.shape[0]
    part_cols = hidden_in.shape[1]
    block_rows = seq_rows // BLK
    work_blocks = grad_qkv.shape[0] // block_rows
    x_rows = hidden_in.astype(jnp.float32)
    local_sq = jnp.sum(x_rows * x_rows, axis=1)
    squares = lax.psum(local_sq, "mp")
    slot_code = block_slot[0]
    in_use = slot_code >= 0
    candidates = REACH * WORKB
    picks = jnp.where(
        in_use[:, None] & (slot_code[:, None] == jnp.arange(candidates)[None, :]), 1.0, 0.0
    )
    picks = picks.astype(jnp.bfloat16)
    work_rows = grad_qkv.reshape(work_blocks, block_rows, grad_qkv.shape[1])
    pieces = [work_rows]
    for offset in range(1, REACH):
        pieces.append(from_behind(work_rows, "dp", -offset))
    stacked = jnp.concatenate(pieces, axis=0)
    chosen = jnp.einsum("bc,crw->brw", picks, stacked, preferred_element_type=jnp.float32)
    own_rows = chosen.astype(jnp.bfloat16).reshape(seq_rows, stacked.shape[2])
    partial_rows = lax.dot_general(
        own_rows,
        lax.all_gather(qkv_weight, "dp", axis=0, tiled=True),
        (((1,), (1,)), ((), ())),
        preferred_element_type=jnp.float32,
    )
    head_rows = lax.psum_scatter(
        partial_rows.astype(jnp.bfloat16), "mp", scatter_dimension=1, tiled=True
    )
    row_index = jnp.arange(seq_rows, dtype=jnp.int32)
    target_rows = jnp.where(row_index < image_count[0], image_pos, seq_rows)
    head_grad = (
        jnp.zeros((seq_rows, part_cols), jnp.float32)
        .at[target_rows]
        .add(head_rows.astype(jnp.float32), mode="drop")
    )
    scaled = head_grad * norm_gain[None, :]
    local_cross = jnp.sum(scaled * x_rows, axis=1)
    cross_sum = lax.psum(local_cross, "mp")
    inv_rms = lax.rsqrt(squares / D + 1e-05)
    result = (
        grad_out.astype(jnp.float32)
        + inv_rms[:, None] * scaled
        - x_rows * (inv_rms**3 * cross_sum / D)[:, None]
    )
    return result.astype(jnp.bfloat16)


def solution(mesh):
    return jax.shard_map(
        shards,
        mesh=mesh,
        in_specs=(
            P("dp", "mp"),
            P("dp", "mp"),
            P("dp", "mp"),
            P("dp", "mp"),
            P("mp"),
            P("dp"),
            P("dp"),
            P("dp", None),
        ),
        out_specs=P("dp", "mp"),
        check_vma=False,
    )
```

profile of v0, /device:TPU:1, one launch (start us, length us, event | category | flops | bytes accessed | tf_op | source)
XLA Modules:
  0.0 271.0 jit_solution(14901396754480817605)
XLA Ops:
  6.5 0.7 all-gather.2.cloned.1.call-update
  7.3 0.0 reduce-scatter.2.cloned.1.call-start
  7.3 1.9 copy.12
  9.2 8.8 %collective-permute-start = (bf16[2,128,1536]{2,0,1:T(2,128)(2,1)S(1)}, bf16[2,128,1536]{2,0,1:T(2,128)(2,1)S(1)}, u32[]{:S(2)}, u32[]{:S(2)}) collective-permute-start(bf16[2,128,1536]{2,0,1:T(2,128)(2,1)S(1)} %copy.12), channel_id=1, source_target_pairs={{4,0},{8,4},{12,8},{16,12},{20,16},{24,20},{28,24},{32,28},{36,32}... | collective-permute-start | bytes 2359304 | tf_op jit(solution)/shard_map/ppermute | solution.py:15
  18.0 8.2 %collective-permute-start.1 = (bf16[2,128,1536]{2,0,1:T(2,128)(2,1)S(1)}, bf16[2,128,1536]{2,0,1:T(2,128)(2,1)S(1)}, u32[]{:S(2)}, u32[]{:S(2)}) collective-permute-start(bf16[2,128,1536]{2,0,1:T(2,128)(2,1)S(1)} %copy.12), channel_id=1, source_target_pairs={{8,0},{12,4},{16,8},{20,12},{24,16},{28,20},{32,24},{36,28},{40,32... | collective-permute-start | bytes 2359304 | tf_op jit(solution)/shard_map/ppermute | solution.py:15
  26.2 2.5 collective-permute-start.2
  28.8 0.7 broadcast_compare_fusion
  29.5 0.0 collective-permute-done
  29.5 23.2 %collective-permute-done.1 = bf16[2,128,1536]{2,0,1:T(2,128)(2,1)S(1)} collective-permute-done((bf16[2,128,1536]{2,0,1:T(2,128)(2,1)S(1)}, bf16[2,128,1536]{2,0,1:T(2,128)(2,1)S(1)}, u32[]{:S(2)}, u32[]{:S(2)}) %collective-permute-start.1) | collective-permute-done | bytes 786464 | tf_op jit(solution)/shard_map/ppermute | solution.py:15
  52.7 19.1 %collective-permute-done.2 = bf16[2,128,1536]{2,0,1:T(2,128)(2,1)S(1)} collective-permute-done((bf16[2,128,1536]{2,0,1:T(2,128)(2,1)S(1)}, bf16[2,128,1536]{2,0,1:T(2,128)(2,1)S(1)}, u32[]{:S(2)}, u32[]{:S(2)}) %collective-permute-start.2) | collective-permute-done | bytes 786464 | tf_op jit(solution)/shard_map/ppermute | solution.py:15
  71.8 4.5 %fusion.8 = bf16[4,128,1536]{2,0,1:T(4,128)(2,1)S(1)} fusion(bf16[2,128,1536]{2,0,1:T(2,128)(2,1)S(1)} %collective-permute-done.2, bf16[2,128,1536]{2,0,1:T(2,128)(2,1)S(1)} %collective-permute-done.1, bf16[2,128,1536]{2,0,1:T(2,128)(2,1)S(1)} %collective-permute-done, bf16[2,128,1536]{2,0,1:T(2,128)(2,1)S(1)} %copy.12, s32[4]{0:T(128)} %bitcast.13, ...), kind=kOutput, calls=%fused_computation.13 | convolution fusion | flops 25952384 | bytes 4718612 | tf_op jit(solution)/shard_map/bc,crw->brw/dot_general | solution.py:40
  76.4 0.3 copy.13
  76.6 103.9 %all-gather.2.cloned.1.call-done = bf16[4096,1536]{1,0:T(8,128)(2,1)} async-done(((bf16[32,1536]{1,0:T(8,128)(2,1)}), bf16[4096,1536]{1,0:T(8,128)(2,1)}) %all-gather.2.cloned.1.call-update) | async-done | bytes 12582928 | tf_op jit(solution)/shard_map/all_gather | solution.py:44
  180.5 18.3 %convolution_convert_fusion = bf16[512,4096]{1,0:T(8,128)(2,1)} fusion(bf16[512,1536]{1,0:T(8,128)(2,1)S(1)} %bitcast.11, bf16[4096,1536]{1,0:T(8,128)(2,1)} %all-gather.2.cloned.1.call-done), kind=kOutput, calls=%fused_computation.1 | convolution fusion | flops 6444548096 | bytes 18350080 | tf_op jit(solution)/shard_map/dot_general | solution.py:42
  198.8 0.0 reduce-scatter.2.cloned.1.call-update
  198.8 0.0 copy-start
  198.9 0.0 copy-start.1
  199.6 0.0 copy-done.2
  199.6 48.6 %reduce-scatter.2.cloned.1.call-done = bf16[512,1024]{1,0:T(8,128)(2,1)} async-done(((bf16[512,4096]{1,0:T(8,128)(2,1)}), bf16[512,1024]{1,0:T(8,128)(2,1)}) %reduce-scatter.2.cloned.1.call-update) | async-done | bytes 1048592 | tf_op jit(solution)/shard_map/reduce_scatter | solution.py:48
  248.2 6.0 %scatter_custom_fusion = f32[512,1024]{1,0:T(8,128)S(1)} fusion(s32[512]{0:T(512)S(1)} %compare_select_fusion, bf16[512,1024]{1,0:T(8,128)(2,1)} %reduce-scatter.2.cloned.1.call-done, f32[]{:T(128)} %constant.6.clone.1), kind=kCustom, calls=%fused_computation.18 | custom fusion | flops 1048576 | bytes 3145732 | tf_op jit(solution)/shard_map/scatter-add | solution.py:56
  254.2 0.0 copy-done
  254.2 0.6 fusion.11
  254.8 6.6 %all-reduce = (f32[512]{0:T(512)S(1)}, f32[512]{0:T(512)S(1)}) all-reduce(f32[512]{0:T(512)S(1)} %get-tuple-element.6, f32[512]{0:T(512)S(1)} %get-tuple-element.5), channel_id=1, replica_groups=mesh['dp'=128,'mp'=4] {'mp'}, use_global_device_ids=true, to_apply=%region_5.6 | all-reduce | flops 1024 | bytes 8192 | tf_op jit(solution)/shard_map/psum | solution.py:60
  261.4 2.8 %fusion.14 = bf16[512,1024]{1,0:T(8,128)(2,1)} fusion(bf16[512,1024]{1,0:T(8,128)(2,1)S(1)} %copy-done, bf16[512,1024]{1,0:T(8,128)(2,1)} %param.9, f32[512,1024]{1,0:T(8,128)S(1)} %scatter_custom_fusion, f32[512]{0:T(512)S(1)} %get-tuple-element.10, f32[1024]{0:T(1024)S(1)} %copy-done.1, f32[512]{0:T(512)S(1)} %get-tuple-element.9), kind=kLoop, calls=%fused_computation.17 | loop fusion | flops 4194304 | bytes 5251072 | tf_op jit(solution)/shard_map/convert_element_type | solution.py:67
  (5 shorter events, 0.0 us)
Async XLA Ops:
  6.5 174.0 %all-gather.2.cloned.1.call-start = ((), (), s32[]{:S(2)}) async-start(), calls=%async_computation.1 | async-start | bytes 12681216 | tf_op jit(solution)/shard_map/all_gather | solution.py:44
  7.3 241.0 %reduce-scatter.2.cloned.1.call-start = ((), (), s32[]{:S(2)}) async-start(), calls=%async_computation.2 | async-start | bytes 5242880 | tf_op jit(solution)/shard_map/reduce_scatter | solution.py:48
  9.2 20.2 %collective-permute-start = (bf16[2,128,1536]{2,0,1:T(2,128)(2,1)S(1)}, bf16[2,128,1536]{2,0,1:T(2,128)(2,1)S(1)}, u32[]{:S(2)}, u32[]{:S(2)}) collective-permute-start(bf16[2,128,1536]{2,0,1:T(2,128)(2,1)S(1)} %copy.12), channel_id=1, source_target_pairs={{4,0},{8,4},{12,8},{16,12},{20,16},{24,20},{28,24},{32,28},{36,32}... | collective-permute-start | bytes 2359304 | tf_op jit(solution)/shard_map/ppermute | solution.py:15
  18.0 34.7 %collective-permute-start.1 = (bf16[2,128,1536]{2,0,1:T(2,128)(2,1)S(1)}, bf16[2,128,1536]{2,0,1:T(2,128)(2,1)S(1)}, u32[]{:S(2)}, u32[]{:S(2)}) collective-permute-start(bf16[2,128,1536]{2,0,1:T(2,128)(2,1)S(1)} %copy.12), channel_id=1, source_target_pairs={{8,0},{12,4},{16,8},{20,12},{24,16},{28,20},{32,24},{36,28},{40,32... | collective-permute-start | bytes 2359304 | tf_op jit(solution)/shard_map/ppermute | solution.py:15
  26.2 45.6 %collective-permute-start.2 = (bf16[2,128,1536]{2,0,1:T(2,128)(2,1)S(1)}, bf16[2,128,1536]{2,0,1:T(2,128)(2,1)S(1)}, u32[]{:S(2)}, u32[]{:S(2)}) collective-permute-start(bf16[2,128,1536]{2,0,1:T(2,128)(2,1)S(1)} %copy.12), channel_id=1, source_target_pairs={{12,0},{16,4},{20,8},{24,12},{28,16},{32,20},{36,24},{40,28},{44,3... | collective-permute-start | bytes 2359304 | tf_op jit(solution)/shard_map/ppermute | solution.py:15
  198.8 0.8 copy-start.2
  198.8 55.3 %copy-start = (bf16[512,1024]{1,0:T(8,128)(2,1)S(1)}, bf16[512,1024]{1,0:T(8,128)(2,1)}, u32[]{:S(2)}) copy-start(bf16[512,1024]{1,0:T(8,128)(2,1)} %param.8) | copy-start | bytes 3145732
  198.9 55.3 %copy-start.1 = (f32[1024]{0:T(1024)S(1)}, f32[1024]{0:T(1024)}, u32[]{:S(2)}) copy-start(f32[1024]{0:T(1024)} %param.12) | copy-start | bytes 12292
Sparse Core Ops, SparseCore 0:
  10.5 169.9 all-gather.1
  199.0 49.2 reduce-scatter.1
where the time goes:
time: 272 us; the launch traced here: 271 us
  waiting for transfers between devices  196 us (72%)
  matrix products  22.8 us (8%)
  starting transfers between devices  19.6 us (7%)
  between operations  14.2 us (5%)
  other arithmetic  10 us (4%)
  blocking collectives  6.58 us (2%)
    all_gather x1, waiting for transfers between devices, shards(): lax.all_gather(qkv_weight, 'dp', axis=0, tiled=True)  104 us
    reduce_scatter x1, waiting for transfers between devices, shards(): lax.psum_scatter(partial_rows.astype(jnp.bfloat16), 'mp', scatter_dimensi...  48.6 us
    ppermute x3, waiting for transfers between devices, from_behind(): return lax.ppermute(block, axis, route)  42.4 us
    ppermute x3, starting transfers between devices, from_behind(): return lax.ppermute(block, axis, route)  19.5 us
    dot_general x1, matrix products, shards(): lax.dot_general(own_rows, lax.all_gather(qkv_weight, 'dp', axis=0, tiled=...  18.3 us
    psum x1, blocking collectives, shards(): cross_sum = lax.psum(local_cross, 'mp')  6.58 us
    scatter-add x1, other arithmetic, shards(): head_grad = jnp.zeros((seq_rows, part_cols), jnp.float32).at[target_rows]...  5.97 us
  transfers between devices with their start and end apart: 5, of which 4 were waited for; matrix products, arithmetic and copies ran while one was open for 3% of the time, Pallas kernels for 0%

commit v1 on v0

v1 whole, which is shorter than its diff:
```python
import functools

import jax
import jax.numpy as jnp
from jax import lax
from jax.experimental import pallas as pl
from jax.experimental.pallas import tpu as pltpu
from jax.sharding import PartitionSpec as P

D = 4096
BLK = 4
REACH = 4
WORKB = 2
NY = 4
NC = 2
PLANE = NY * NC
MESH = pl.DeviceIdType.MESH
NT = (((1,), (1,)), ((), ()))


def kernel(
    nz, nx, slot_ref, c_ref, w_ref, tgt_ref, out_ref,
    cg, wg, ps, xr, sb, rb, rows, perm,
    c_send, c_recv, w_send, w_recv, x_send, x_recv, s_send, s_recv, own_sem,
):
    br = c_ref.shape[0] // WORKB
    wr = w_ref.shape[0]
    pn = ps.shape[3]
    me = lax.axis_index("dp")
    x = lax.axis_index("mp")
    z, lane = me // PLANE, lax.rem(me, PLANE)
    y, c = lane // NC, lax.rem(lane, NC)
    shards = nz * PLANE
    yp, ym, y2 = lax.rem(y + 1, NY), lax.rem(y + 3, NY), lax.rem(y + 2, NY)
    plane = z * PLANE
    sibling = plane + y * NC + 1 - c
    above, below = plane + yp * NC + c, plane + ym * NC + c
    z_up, z_down = lax.rem(me + PLANE, shards), lax.rem(me + shards - PLANE, shards)

    def remote(src, dst, send, recv, dp_to, x_to):
        return pltpu.make_async_remote_copy(
            src_ref=src, dst_ref=dst, send_sem=send, recv_sem=recv,
            device_id=(dp_to, x_to), device_id_type=MESH,
        )

    def landed(dst, recv):
        remote(dst, dst, own_sem.at[0], recv, sibling, x).wait_recv()

    barrier = pltpu.get_barrier_semaphore()

    def greet(dp_to, x_to):
        pl.semaphore_signal(barrier, inc=1, device_id=(dp_to, x_to), device_id_type=MESH)

    greet(z_up, x)
    greet(z_down, x)
    for r in range(1, PLANE):
        greet(plane + lax.rem(lane + r, PLANE), x)
    for r in range(1, nx):
        greet(me, lax.rem(x + r, nx))
    for r in range(1, REACH):
        greet(lax.rem(plane + shards - r, shards), x)

    @pl.when(lane >= PLANE - REACH + 1)
    def _():
        for r in range(PLANE):
            greet(lax.rem(plane + PLANE + r, shards), x)

    peers = 2 + (PLANE - 1) + (nx - 1) + (REACH - 1)
    pl.semaphore_wait(barrier, jnp.where(lane >= PLANE - REACH + 1, peers + PLANE, peers))

    pending = []

    def go(copy):
        copy.start()
        pending.append(copy)

    def slot_at(yy, cc, h):
        return cg.at[yy, pl.ds(pl.multiple_of((cc * WORKB + h) * br, 16), br)]

    def slot_sem(yy, cc, h):
        return c_recv.at[(yy * NC + cc) * WORKB + h]

    def own_half(h):
        return c_ref.at[pl.ds(h * br, br)]

    def w_at(zz):
        return wg.at[pl.ds(pl.multiple_of(zz * wr, 16), wr)]

    sends = 0
    for h, to in ((0, above), (1, below), (1, above), (0, below), (0, sibling), (1, sibling)):
        go(remote(own_half(h), slot_at(y, c, h), c_send.at[sends], slot_sem(y, c, h), to, x))
        sends += 1
    up_steps = nz // 2
    down_steps = nz - 1 - up_steps
    go(remote(w_ref, w_at(z), w_send.at[0], w_recv.at[z], z_up, x))
    go(remote(w_ref, w_at(z), w_send.at[nz], w_recv.at[z], z_down, x))
    own_c = pltpu.make_async_copy(c_ref, cg.at[y, pl.ds(pl.multiple_of(c * WORKB * br, 16), WORKB * br)], own_sem.at[0])
    own_w = pltpu.make_async_copy(w_ref, w_at(z), own_sem.at[1])
    own_c.start()
    own_w.start()

    width = perm.shape[0]
    src = lax.broadcasted_iota(jnp.int32, (width, 1), 0)
    goes_to = (lax.rem(src, pn) // wr) * (PLANE * wr) + (src // pn) * wr + lax.rem(src, wr)
    perm[...] = (goes_to == lax.broadcasted_iota(jnp.int32, (width, width), 1)).astype(jnp.float32).astype(jnp.bfloat16)
    own_c.wait()
    own_w.wait()

    def w_step(k):
        zz = lax.rem(z + nz - k, nz)
        landed(w_at(zz), w_recv.at[zz])
        if k < up_steps:
            go(remote(w_at(zz), w_at(zz), w_send.at[k], w_recv.at[zz], z_up, x))
        if k <= down_steps:
            zz = lax.rem(z + k, nz)
            landed(w_at(zz), w_recv.at[zz])
            if k < down_steps:
                go(remote(w_at(zz), w_at(zz), w_send.at[nz + k], w_recv.at[zz], z_down, x))

    def pass_on(yy, h, to=None):
        nonlocal sends
        landed(slot_at(yy, c, h), slot_sem(yy, c, h))
        for dest in ([] if to is None else [to]) + [sibling]:
            go(remote(slot_at(yy, c, h), slot_at(yy, c, h), c_send.at[sends], slot_sem(yy, c, h), dest, x))
            sends += 1

    def multiply(k, yy):
        for h in range(WORKB):
            landed(slot_at(yy, 1 - c, h), slot_sem(yy, 1 - c, h))

        @pl.loop(0, NC)
        def _(half):
            at = pl.ds(pl.multiple_of(half * WORKB * br, 16), WORKB * br)
            part = lax.dot_general(cg[yy, at], wg[...], NT, preferred_element_type=jnp.float32)
            part = part.astype(jnp.bfloat16)
            for xx in range(nx):
                ps[xx, yy, at] = part[:, xx * pn:(xx + 1) * pn]

        for r in range(1, nx):
            xx = lax.rem(x + r, nx)
            i = k * (nx - 1) + r - 1
            go(remote(ps.at[xx, yy], xr.at[r - 1, yy], x_send.at[i], x_recv.at[i], me, xx))

    def combine(k, yy):
        total = ps[x, yy].astype(jnp.float32)
        for r in range(1, nx):
            landed(xr.at[r - 1, yy], x_recv.at[k * (nx - 1) + r - 1])
            total = total + xr[r - 1, yy].astype(jnp.float32)
        total = total.astype(jnp.bfloat16)
        for s in range(NC * WORKB):
            sb[yy, s] = total[s * br:(s + 1) * br]
        for cc in range(NC):
            for o in range(REACH):
                dest = dest_of(yy, cc, o)

                @pl.when(dest == me)
                def _():
                    pltpu.make_async_copy(*route(yy, cc, o)).start()

                @pl.when(dest != me)
                def _():
                    deliver(k, yy, cc, o).start()

    def dest_of(yy, cc, o):
        return lax.rem(plane + yy * NC + cc - o + shards, shards)

    def route(yy, cc, o):
        from_ref = sb.at[yy, pl.ds(cc * WORKB, WORKB)]
        return from_ref, rb.at[lane, pl.ds(o * WORKB, WORKB)], s_recv.at[lane * REACH + o]

    def deliver(k, yy, cc, o):
        from_ref, to_ref, recv = route(yy, cc, o)
        return remote(from_ref, to_ref, s_send.at[(k * NC + cc) * REACH + o], recv, dest_of(yy, cc, o), x)

    order = [y, ym, yp, y2]
    for k in range(1, up_steps + 1):
        w_step(k)
        if k == up_steps // 2:
            pass_on(ym, 0, above)
            pass_on(yp, 1, below)
    multiply(0, order[0])
    pass_on(ym, 1)
    pass_on(yp, 0)
    multiply(1, order[1])
    multiply(2, order[2])
    combine(0, order[0])
    pass_on(y2, 0)
    pass_on(y2, 1)
    combine(1, order[1])
    multiply(3, order[3])
    combine(2, order[2])
    combine(3, order[3])

    for s in range(PLANE):
        for o in range(REACH):
            landed(rb.at[s, pl.ds(o * WORKB, WORKB)], s_recv.at[s * REACH + o])
    for b in range(BLK):
        v = slot_ref[0, b]
        used = v >= 0
        pick = jnp.maximum(v, 0)
        for s in range(PLANE):
            block = rb[s, pick]
            rows[b * br:(b + 1) * br, s * pn:(s + 1) * pn] = jnp.where(used, block, jnp.zeros_like(block))
    seq = BLK * br
    place = (lax.broadcasted_iota(jnp.int32, (seq, seq), 0) == tgt_ref[...]).astype(jnp.float32).astype(jnp.bfloat16)
    placed = jnp.dot(place, rows[...], preferred_element_type=jnp.float32).astype(jnp.bfloat16)
    out_ref[...] = jnp.dot(placed, perm[...], preferred_element_type=jnp.float32).astype(jnp.bfloat16)

    for copy in pending:
        copy.wait_send()
    for k in range(NY):
        for cc in range(NC):
            for o in range(REACH):
                @pl.when(dest_of(order[k], cc, o) != me)
                def _():
                    deliver(k, order[k], cc, o).wait_send()


def shards(nz, nx, hidden_in, grad_out, grad_qkv, qkv_weight, norm_gain, image_count, image_pos, block_slot):
    seq, cols = hidden_in.shape
    br = seq // BLK
    depth = grad_qkv.shape[1]
    wr = qkv_weight.shape[0]
    pn = nz * wr // nx
    row_index = jnp.arange(seq, dtype=jnp.int32)
    target = jnp.where(row_index < image_count[0], image_pos, seq)[None, :]
    bf16 = jnp.bfloat16
    dma = pltpu.SemaphoreType.DMA
    vmem = pl.BlockSpec(memory_space=pltpu.VMEM)
    head_grad = pl.pallas_call(
        functools.partial(kernel, nz, nx),
        out_shape=jax.ShapeDtypeStruct((seq, cols), bf16),
        in_specs=[pl.BlockSpec(memory_space=pltpu.SMEM), vmem, vmem, vmem],
        out_specs=vmem,
        scratch_shapes=[
            pltpu.VMEM((NY, NC * WORKB * br, depth), bf16),
            pltpu.VMEM((nz * wr, depth), bf16),
            pltpu.VMEM((nx, NY, NC * WORKB * br, pn), bf16),
            pltpu.VMEM((nx - 1, NY, NC * WORKB * br, pn), bf16),
            pltpu.VMEM((NY, NC * WORKB, br, pn), bf16),
            pltpu.VMEM((PLANE, REACH * WORKB, br, pn), bf16),
            pltpu.VMEM((seq, cols), bf16),
            pltpu.VMEM((cols, cols), bf16),
            dma((14,)),
            dma((PLANE * WORKB,)),
            dma((2 * nz,)),
            dma((nz,)),
            dma((NY * (nx - 1),)),
            dma((NY * (nx - 1),)),
            dma((PLANE * REACH,)),
            dma((PLANE * REACH,)),
            dma((2,)),
        ],
        compiler_params=pltpu.CompilerParams(
            collective_id=0, has_side_effects=True, vmem_limit_bytes=44 * 1024 * 1024
        ),
    )(block_slot, grad_qkv, qkv_weight, target)

    x_rows = hidden_in.astype(jnp.float32)
    scaled = head_grad.astype(jnp.float32) * norm_gain[None, :]
    local = jnp.stack([jnp.sum(x_rows * x_rows, axis=1), jnp.sum(scaled * x_rows, axis=1)])
    squares, cross = lax.psum(local, "mp")
    inv_rms = lax.rsqrt(squares / D + 1e-05)
    result = (
        grad_out.astype(jnp.float32)
        + inv_rms[:, None] * scaled
        - x_rows * (inv_rms**3 * cross / D)[:, None]
    )
    return result.astype(bf16)


def solution(mesh):
    nz, nx = mesh.shape["dp"] // PLANE, mesh.shape["mp"]
    return jax.shard_map(
        functools.partial(shards, nz, nx),
        mesh=mesh,
        in_specs=(
            P("dp", "mp"),
            P("dp", "mp"),
            P("dp", "mp"),
            P("dp", "mp"),
            P("mp"),
            P("dp"),
            P("dp"),
            P("dp", None),
        ),
        out_specs=P("dp", "mp"),
        check_vma=False,
    )
```

time: 272 us -> 102 us (0.38)
  the two profiles are of different devices: /device:TPU:1 before, /device:TPU:2 now
where the time goes in v1:
time: 102 us
  Pallas kernels  85.6 us (84%)
  blocking collectives  9.69 us (10%)
  other arithmetic  2.89 us (3%)
  local copies, waits for them, and re-layouts  2.69 us (3%)
    pallas_call x1, Pallas kernels, shards(): pl.pallas_call(functools.partial(kernel, nz, nx), out_shape=jax.ShapeDtyp...  85.6 us
    psum x1, blocking collectives, shards(): squares, cross = lax.psum(local, 'mp')  9.69 us
    unnamed x12, local copies, waits for them, and re-layouts  2.69 us

profile of v1, /device:TPU:2, one launch (start us, length us, event | category | flops | bytes accessed | tf_op | source)
XLA Modules:
  0.0 101.6 jit_solution(9655781420204109764)
XLA Ops:
  0.0 0.0 copy-start.5
  0.7 0.7 fusion.8
  1.4 0.0 copy-start
  1.4 1.1 %copy-done = bf16[256,1536]{1,0:T(8,128)(2,1)S(1)} copy-done((bf16[256,1536]{1,0:T(8,128)(2,1)S(1)}, bf16[256,1536]{1,0:T(8,128)(2,1)}, u32[]{:S(2)}) %copy-start) | copy-done | bytes 786456
  2.5 0.0 copy-start.1
  2.5 0.9 copy-done.1
  3.4 0.0 copy-start.2
  3.4 0.7 copy-done.2
  4.0 0.0 copy-start.3
  4.0 85.6 %shard_map.82 = bf16[512,1024]{1,0:T(8,128)(2,1)S(1)} custom-call(s32[1,4]{1,0:T(1,128)S(1)} %copy-done.2, bf16[256,1536]{1,0:T(8,128)(2,1)S(1)} %copy-done, bf16[32,1536]{1,0:T(8,128)(2,1)S(1)} %copy-done.1, s32[1,512]{1,0:T(1,128)S(1)} %bitcast.7), custom_call_target="tpu_custom_call" | custom-call | tf_op jit(solution)/shard_map/pallas_call | solution.py:230
  89.7 0.0 copy-done.5
  89.7 0.0 copy-done.3
  89.7 0.0 copy-start.4
  89.7 0.6 fusion
  90.3 9.7 %psum.7 = f32[2,512]{1,0:T(2,128)S(1)} all-reduce(f32[2,512]{1,0:T(2,128)S(1)} %pad_maximum_fusion), channel_id=1, replica_groups=mesh['dp'=128,'mp'=4] {'mp'}, use_global_device_ids=true, to_apply=%region_2.3 | all-reduce | flops 1024 | bytes 8192 | tf_op jit(solution)/shard_map/psum | solution.py:262
  100.0 0.0 copy-done.4
  100.0 1.6 %fusion.3 = bf16[512,1024]{1,0:T(8,128)(2,1)} fusion(bf16[512,1024]{1,0:T(8,128)(2,1)S(1)} %copy-done.3, bf16[512,1024]{1,0:T(8,128)(2,1)S(1)} %shard_map.82, bf16[512,1024]{1,0:T(8,128)(2,1)S(1)} %copy-done.4, f32[512]{0:T(512)S(1)} %fusion.5, f32[512]{0:T(512)S(1)} %bitcast.9, f32[1024]{0:T(1024)S(1)} %copy-done.5), kind=kLoop, calls=%fused_computation.6 | loop fusion | flops 4718592 | bytes 4202496 | tf_op jit(solution)/shard_map/convert_element_type | solution.py:269
  (3 shorter events, 0.0 us)
Async XLA Ops:
  0.0 89.7 %copy-start.5 = (f32[1024]{0:T(1024)S(1)}, f32[1024]{0:T(1024)}, u32[]{:S(2)}) copy-start(f32[1024]{0:T(1024)} %param.12) | copy-start | bytes 12292
  1.4 1.1 %copy-start = (bf16[256,1536]{1,0:T(8,128)(2,1)S(1)}, bf16[256,1536]{1,0:T(8,128)(2,1)}, u32[]{:S(2)}) copy-start(bf16[256,1536]{1,0:T(8,128)(2,1)} %c_ref.1) | copy-start | bytes 2359300
  2.5 0.9 copy-start.1
  3.4 0.7 copy-start.2
  4.0 85.7 %copy-start.3 = (bf16[512,1024]{1,0:T(8,128)(2,1)S(1)}, bf16[512,1024]{1,0:T(8,128)(2,1)}, u32[]{:S(2)}) copy-start(bf16[512,1024]{1,0:T(8,128)(2,1)} %param.8) | copy-start | bytes 3145732
  89.7 10.3 %copy-start.4 = (bf16[512,1024]{1,0:T(8,128)(2,1)S(1)}, bf16[512,1024]{1,0:T(8,128)(2,1)}, u32[]{:S(2)}) copy-start(bf16[512,1024]{1,0:T(8,128)(2,1)} %param.9) | copy-start | bytes 3145732

commit v2 on v1

v2 whole, which is shorter than its diff:
```python
import functools

import jax
import jax.numpy as jnp
from jax import lax
from jax.experimental import pallas as pl
from jax.experimental.pallas import tpu as pltpu
from jax.sharding import PartitionSpec as P

D = 4096
BLK = 4
REACH = 4
WORKB = 2
NY = 4
NC = 2
PLANE = NY * NC
WCUT = 2
MESH = pl.DeviceIdType.MESH
NT = (((1,), (1,)), ((), ()))


def kernel(
    nz, nx, slot_ref, count_ref, pos_ref, gain_ref, hid_ref, c_ref, w_ref, grad_ref, stat_ref,
    cg, wg, ps, xr, sb, rb, rt, hid, stats,
    c_send, c_recv, w_send, w_recv, x_send, x_recv, s_send, s_recv, t_send, t_recv, own_sem,
):
    br = c_ref.shape[0] // WORKB
    wr, depth = w_ref.shape
    pn = ps.shape[2]
    me = lax.axis_index("dp")
    x = lax.axis_index("mp")
    z, lane = me // PLANE, lax.rem(me, PLANE)
    y, c = lane // NC, lax.rem(lane, NC)
    shards = nz * PLANE
    yp, ym, y2 = lax.rem(y + 1, NY), lax.rem(y + 3, NY), lax.rem(y + 2, NY)
    plane = z * PLANE
    sibling = plane + y * NC + 1 - c
    above, below = plane + yp * NC + c, plane + ym * NC + c
    z_up, z_down = lax.rem(me + PLANE, shards), lax.rem(me + shards - PLANE, shards)

    def remote(src, dst, send, recv, dp_to, x_to):
        return pltpu.make_async_remote_copy(
            src_ref=src, dst_ref=dst, send_sem=send, recv_sem=recv,
            device_id=(dp_to, x_to), device_id_type=MESH,
        )

    def landed(dst, recv):
        remote(dst, dst, own_sem.at[0], recv, sibling, x).wait_recv()

    barrier = pltpu.get_barrier_semaphore()

    def greet(dp_to, x_to):
        pl.semaphore_signal(barrier, inc=1, device_id=(dp_to, x_to), device_id_type=MESH)

    greet(z_up, x)
    greet(z_down, x)
    for r in range(1, PLANE):
        greet(plane + lax.rem(lane + r, PLANE), x)
    for r in range(1, nx):
        greet(me, lax.rem(x + r, nx))
    for r in range(1, REACH):
        greet(lax.rem(plane + shards - r, shards), x)

    @pl.when(lane >= PLANE - REACH + 1)
    def _():
        for r in range(PLANE):
            greet(lax.rem(plane + PLANE + r, shards), x)

    def w_part(ref, base, p):
        at = base + (p // WCUT) * (wr // WCUT)
        return ref.at[pl.ds(pl.multiple_of(at, 16), wr // WCUT), pl.ds((p % WCUT) * (depth // WCUT), depth // WCUT)]

    own_c = pltpu.make_async_copy(c_ref, cg.at[y, pl.ds(pl.multiple_of(c * WORKB * br, 16), WORKB * br)], own_sem.at[0])
    own_w = pltpu.make_async_copy(w_ref, wg.at[pl.ds(pl.multiple_of(z * wr, 16), wr)], own_sem.at[1])
    own_h = pltpu.make_async_copy(hid_ref, hid, own_sem.at[2])
    own_c.start()
    own_w.start()
    own_h.start()
    peers = 2 + (PLANE - 1) + (nx - 1) + (REACH - 1)
    pl.semaphore_wait(barrier, jnp.where(lane >= PLANE - REACH + 1, peers + PLANE, peers))

    pending = []

    def go(copy):
        copy.start()
        pending.append(copy)

    def slot_at(yy, cc, h):
        return cg.at[yy, pl.ds(pl.multiple_of((cc * WORKB + h) * br, 16), br)]

    def slot_sem(yy, cc, h):
        return c_recv.at[(yy * NC + cc) * WORKB + h]

    def own_half(h):
        return c_ref.at[pl.ds(h * br, br)]

    parts = WCUT * WCUT
    up_steps = nz // 2
    down_steps = nz - 1 - up_steps

    def w_go(src, zz, p, k, up):
        send = w_send.at[((0 if up else nz) + k) * parts + p]
        go(remote(src, w_part(wg, zz * wr, p), send, w_recv.at[zz * parts + p], z_up if up else z_down, x))

    sends = 0
    for p in range(parts):
        w_go(w_part(w_ref, 0, p), z, p, 0, True)
        w_go(w_part(w_ref, 0, p), z, p, 0, False)
    for h, to in ((0, above), (1, below), (1, above), (0, below), (0, sibling), (1, sibling)):
        go(remote(own_half(h), slot_at(y, c, h), c_send.at[sends], slot_sem(y, c, h), to, x))
        sends += 1

    def row_sums(value):
        lanes = value[:, :128]
        for t in range(1, value.shape[1] // 128):
            lanes = lanes + value[:, t * 128:(t + 1) * 128]
        return jnp.sum(lanes.T, axis=0, keepdims=True)

    own_c.wait()
    own_w.wait()
    own_h.wait()
    h_rows = hid[...].astype(jnp.float32)
    stats[0] = jnp.zeros(stats.shape[1:], jnp.float32)
    stats[0, 0:1, :] = row_sums(h_rows * h_rows)

    def w_step(k):
        for p in range(parts):
            zz = lax.rem(z + nz - k, nz)
            landed(w_part(wg, zz * wr, p), w_recv.at[zz * parts + p])
            if k < up_steps:
                w_go(w_part(wg, zz * wr, p), zz, p, k, True)
            if k <= down_steps:
                zz = lax.rem(z + k, nz)
                landed(w_part(wg, zz * wr, p), w_recv.at[zz * parts + p])
                if k < down_steps:
                    w_go(w_part(wg, zz * wr, p), zz, p, k, False)

    def pass_on(yy, h, to=None):
        nonlocal sends
        landed(slot_at(yy, c, h), slot_sem(yy, c, h))
        for dest in ([] if to is None else [to]) + [sibling]:
            go(remote(slot_at(yy, c, h), slot_at(yy, c, h), c_send.at[sends], slot_sem(yy, c, h), dest, x))
            sends += 1

    def multiply(k, yy):
        for h in range(WORKB):
            landed(slot_at(yy, 1 - c, h), slot_sem(yy, 1 - c, h))

        @pl.loop(0, nx)
        def _(xx):
            at = pl.ds(pl.multiple_of(xx * pn, 16), pn)
            part = lax.dot_general(wg[at], cg[yy], NT, preferred_element_type=jnp.float32)
            ps[xx, yy] = part.astype(jnp.bfloat16)

        for r in range(1, nx):
            xx = lax.rem(x + r, nx)
            i = k * (nx - 1) + r - 1
            go(remote(ps.at[xx, yy], xr.at[r - 1, yy], x_send.at[i], x_recv.at[i], me, xx))

    def combine(k, yy):
        total = ps[x, yy].astype(jnp.float32)
        for r in range(1, nx):
            landed(xr.at[r - 1, yy], x_recv.at[k * (nx - 1) + r - 1])
            total = total + xr[r - 1, yy].astype(jnp.float32)
        total = total.astype(jnp.bfloat16)
        for s in range(NC * WORKB):
            sb[yy, s] = total[:, s * br:(s + 1) * br].reshape(sb.shape[2:])
        for cc in range(NC):
            for o in range(REACH):
                dest = dest_of(yy, cc, o)

                @pl.when(dest == me)
                def _():
                    pltpu.make_async_copy(*route(yy, cc, o)).start()

                @pl.when(dest != me)
                def _():
                    deliver(k, yy, cc, o).start()

    def dest_of(yy, cc, o):
        return lax.rem(plane + yy * NC + cc - o + shards, shards)

    def candidates(o, source):
        return rb.at[pl.ds(o * WORKB, WORKB), :, source]

    def route(yy, cc, o):
        from_ref = sb.at[yy, pl.ds(cc * WORKB, WORKB)]
        return from_ref, candidates(o, lane), s_recv.at[lane * REACH + o]

    def deliver(k, yy, cc, o):
        from_ref, to_ref, recv = route(yy, cc, o)
        return remote(from_ref, to_ref, s_send.at[(k * NC + cc) * REACH + o], recv, dest_of(yy, cc, o), x)

    order = [y, ym, yp, y2]
    for k in range(1, up_steps + 1):
        w_step(k)
        if k == up_steps // 2:
            pass_on(ym, 0, above)
            pass_on(yp, 1, below)
        if k == up_steps - 1:
            pass_on(ym, 1)
            pass_on(yp, 0)
    for k in range(3):
        multiply(k, order[k])
    pass_on(y2, 0)
    pass_on(y2, 1)
    combine(0, order[0])
    multiply(3, order[3])
    for k in range(1, 4):
        combine(k, order[k])

    seq = BLK * br
    target = jnp.where(lax.broadcasted_iota(jnp.int32, (1, seq), 1) < count_ref[0], pos_ref[...], seq)
    place = (lax.broadcasted_iota(jnp.int32, (seq, seq), 0) == target).astype(jnp.float32).astype(jnp.bfloat16)
    for s in range(PLANE):
        for o in range(REACH):
            landed(candidates(o, s), s_recv.at[s * REACH + o])
    for b in range(BLK):
        v = slot_ref[0, b]
        block = rb[jnp.maximum(v, 0)].reshape(rt.shape[0], br)
        rt[:, b * br:(b + 1) * br] = jnp.where(v >= 0, block, jnp.zeros_like(block))
    placed = lax.dot_general(place, rt[...], NT, preferred_element_type=jnp.float32)
    grad_ref[...] = placed.astype(jnp.bfloat16)
    stats[0, 1:2, :] = row_sums(placed * gain_ref[...] * hid[...].astype(jnp.float32))
    for r in range(1, nx):
        go(remote(stats.at[0], stats.at[r], t_send.at[r - 1], t_recv.at[r - 1], me, lax.rem(x + r, nx)))
    total = stats[0]
    for r in range(1, nx):
        landed(stats.at[r], t_recv.at[r - 1])
        total = total + stats[r]
    stat_ref[...] = total

    for copy in pending:
        copy.wait_send()
    for k in range(NY):
        for cc in range(NC):
            for o in range(REACH):
                @pl.when(dest_of(order[k], cc, o) != me)
                def _():
                    deliver(k, order[k], cc, o).wait_send()


def shards(nz, nx, hidden_in, grad_out, grad_qkv, qkv_weight, norm_gain, image_count, image_pos, block_slot):
    seq, cols = hidden_in.shape
    br = seq // BLK
    depth = grad_qkv.shape[1]
    wr = qkv_weight.shape[0]
    pn = nz * wr // nx
    bf16 = jnp.bfloat16
    dma = pltpu.SemaphoreType.DMA
    vmem = pl.BlockSpec(memory_space=pltpu.VMEM)
    smem = pl.BlockSpec(memory_space=pltpu.SMEM)
    hbm = pl.BlockSpec(memory_space=pl.ANY)
    chip_rows = NC * WORKB * br
    parts = WCUT * WCUT
    head_grad, stats = pl.pallas_call(
        functools.partial(kernel, nz, nx),
        out_shape=(jax.ShapeDtypeStruct((seq, cols), bf16), jax.ShapeDtypeStruct((8, seq), jnp.float32)),
        in_specs=[smem, smem, vmem, vmem, hbm, hbm, hbm],
        out_specs=(vmem, vmem),
        scratch_shapes=[
            pltpu.VMEM((NY, chip_rows, depth), bf16),
            pltpu.VMEM((nz * wr, depth), bf16),
            pltpu.VMEM((nx, NY, pn, chip_rows), bf16),
            pltpu.VMEM((nx - 1, NY, pn, chip_rows), bf16),
            pltpu.VMEM((NY, NC * WORKB, nz // nx, wr, br), bf16),
            pltpu.VMEM((REACH * WORKB, nz // nx, PLANE, wr, br), bf16),
            pltpu.VMEM((cols, seq), bf16),
            pltpu.VMEM((seq, cols), bf16),
            pltpu.VMEM((nx, 8, seq), jnp.float32),
            dma((14,)),
            dma((PLANE * WORKB,)),
            dma((2 * nz * parts,)),
            dma((nz * parts,)),
            dma((NY * (nx - 1),)),
            dma((NY * (nx - 1),)),
            dma((PLANE * REACH,)),
            dma((PLANE * REACH,)),
            dma((nx - 1,)),
            dma((nx - 1,)),
            dma((3,)),
        ],
        compiler_params=pltpu.CompilerParams(
            collective_id=0, has_side_effects=True, vmem_limit_bytes=60 * 1024 * 1024
        ),
    )(block_slot, image_count, image_pos[None, :], norm_gain[None, :], hidden_in, grad_qkv, qkv_weight)

    squares, cross = stats[0], stats[1]
    inv_rms = lax.rsqrt(squares / D + 1e-05)
    result = (
        grad_out.astype(jnp.float32)
        + inv_rms[:, None] * (head_grad.astype(jnp.float32) * norm_gain[None, :])
        - hidden_in.astype(jnp.float32) * (inv_rms**3 * cross / D)[:, None]
    )
    return result.astype(bf16)


def solution(mesh):
    nz, nx = mesh.shape["dp"] // PLANE, mesh.shape["mp"]
    return jax.shard_map(
        functools.partial(shards, nz, nx),
        mesh=mesh,
        in_specs=(
            P("dp", "mp"),
            P("dp", "mp"),
            P("dp", "mp"),
            P("dp", "mp"),
            P("mp"),
            P("dp"),
            P("dp"),
            P("dp", None),
        ),
        out_specs=P("dp", "mp"),
        check_vma=False,
    )
```

time: 102 us -> 92.9 us (0.911)
  the two profiles are of different devices: /device:TPU:2 before, /device:TPU:1 now
where the time goes in v2:
time: 92.9 us; the launch traced here: 91.4 us
  Pallas kernels  86.7 us (93%)
  other arithmetic  3.95 us (4%)
    pallas_call x1, Pallas kernels, shards(): pl.pallas_call(functools.partial(kernel, nz, nx), out_shape=(jax.ShapeDty...  86.7 us
    convert_element_type x1, other arithmetic, shards(): return result.astype(bf16)  3.14 us

profile of v2, /device:TPU:1, one launch (start us, length us, event | category | flops | bytes accessed | tf_op | source)
XLA Modules:
  0.0 91.4 jit_solution(4131617962414048892)
XLA Ops:
  0.0 0.0 copy-start.1
  0.0 0.0 copy-start
  0.7 86.7 %shard_map.82 = (bf16[512,1024]{1,0:T(8,128)(2,1)}, f32[8,512]{1,0:T(8,128)}) custom-call(s32[1,4]{1,0:T(1,128)} %slot_ref.1, s32[1]{0:T(128)S(6)} %copy.9.count_ref, s32[1,512]{1,0:T(1,128)} %bitcast.8, f32[1,1024]{1,0:T(1,128)} %bitcast.6, bf16[512,1024]{1,0:T(8,128)(2,1)} %hid_ref.1, bf16[256,1536]{1,0:T(8,128)(2,1)} %c_ref.1, bf16[32,1536]{1,0:T(8,128)(2,1)} %w_ref.1), custom_call_target="tpu_custom_call" | custom-call | tf_op jit(solution)/shard_map/pallas_call | solution.py:256
  87.5 0.8 add_rsqrt_fusion
  88.3 0.0 copy-done.1
  88.3 0.0 copy-done
  88.3 3.1 %subtract_convert_fusion = bf16[512,1024]{1,0:T(8,128)(2,1)} fusion(bf16[512,1024]{1,0:T(8,128)(2,1)S(1)} %copy-done, bf16[512,1024]{1,0:T(8,128)(2,1)} %get-tuple-element.8, bf16[512,1024]{1,0:T(8,128)(2,1)} %param.9, f32[512]{0:T(512)S(1)} %fusion.1, f32[1024]{0:T(1024)S(1)} %copy-done.1, f32[512]{0:T(512)S(1)} %bitcast.5), kind=kLoop, calls=%fused_computation | loop fusion | flops 4718592 | bytes 4202496 | tf_op jit(solution)/shard_map/convert_element_type | solution.py:295
  (1 shorter events, 0.0 us)
Async XLA Ops:
  0.0 88.3 %copy-start.1 = (f32[1024]{0:T(1024)S(1)}, f32[1024]{0:T(1024)}, u32[]{:S(2)}) copy-start(f32[1024]{0:T(1024)} %param.12) | copy-start | bytes 12292
  0.0 88.3 %copy-start = (bf16[512,1024]{1,0:T(8,128)(2,1)S(1)}, bf16[512,1024]{1,0:T(8,128)(2,1)}, u32[]{:S(2)}) copy-start(bf16[512,1024]{1,0:T(8,128)(2,1)} %hid_ref.1) | copy-start | bytes 3145732

commit v3 on v2

--- a/solution.py
+++ b/solution.py
@@ -14,7 +14,8 @@
 NY = 4
 NC = 2
 PLANE = NY * NC
-WCUT = 2
+W_ROW_CUT = 2
+W_COL_CUT = 1
 MESH = pl.DeviceIdType.MESH
 NT = (((1,), (1,)), ((), ()))
 
@@ -58,17 +59,11 @@
         greet(plane + lax.rem(lane + r, PLANE), x)
     for r in range(1, nx):
         greet(me, lax.rem(x + r, nx))
-    for r in range(1, REACH):
-        greet(lax.rem(plane + shards - r, shards), x)
-
-    @pl.when(lane >= PLANE - REACH + 1)
-    def _():
-        for r in range(PLANE):
-            greet(lax.rem(plane + PLANE + r, shards), x)
 
     def w_part(ref, base, p):
-        at = base + (p // WCUT) * (wr // WCUT)
-        return ref.at[pl.ds(pl.multiple_of(at, 16), wr // WCUT), pl.ds((p % WCUT) * (depth // WCUT), depth // WCUT)]
+        tall, wide = wr // W_ROW_CUT, depth // W_COL_CUT
+        at = base + (p // W_COL_CUT) * tall
+        return ref.at[pl.ds(pl.multiple_of(at, 16), tall), pl.ds((p % W_COL_CUT) * wide, wide)]
 
     own_c = pltpu.make_async_copy(c_ref, cg.at[y, pl.ds(pl.multiple_of(c * WORKB * br, 16), WORKB * br)], own_sem.at[0])
     own_w = pltpu.make_async_copy(w_ref, wg.at[pl.ds(pl.multiple_of(z * wr, 16), wr)], own_sem.at[1])
@@ -76,8 +71,7 @@
     own_c.start()
     own_w.start()
     own_h.start()
-    peers = 2 + (PLANE - 1) + (nx - 1) + (REACH - 1)
-    pl.semaphore_wait(barrier, jnp.where(lane >= PLANE - REACH + 1, peers + PLANE, peers))
+    pl.semaphore_wait(barrier, 2 + (PLANE - 1) + (nx - 1))
 
     pending = []
 
@@ -94,7 +88,7 @@
     def own_half(h):
         return c_ref.at[pl.ds(h * br, br)]
 
-    parts = WCUT * WCUT
+    parts = W_ROW_CUT * W_COL_CUT
     up_steps = nz // 2
     down_steps = nz - 1 - up_steps
 
@@ -146,11 +140,9 @@
         for h in range(WORKB):
             landed(slot_at(yy, 1 - c, h), slot_sem(yy, 1 - c, h))
 
-        @pl.loop(0, nx)
-        def _(xx):
-            at = pl.ds(pl.multiple_of(xx * pn, 16), pn)
-            part = lax.dot_general(wg[at], cg[yy], NT, preferred_element_type=jnp.float32)
-            ps[xx, yy] = part.astype(jnp.bfloat16)
+        part = lax.dot_general(wg[...], cg[yy], NT, preferred_element_type=jnp.float32).astype(jnp.bfloat16)
+        for xx in range(nx):
+            ps[xx, yy] = part[xx * pn:(xx + 1) * pn]
 
         for r in range(1, nx):
             xx = lax.rem(x + r, nx)
@@ -191,7 +183,7 @@
         from_ref, to_ref, recv = route(yy, cc, o)
         return remote(from_ref, to_ref, s_send.at[(k * NC + cc) * REACH + o], recv, dest_of(yy, cc, o), x)
 
-    order = [y, ym, yp, y2]
+    order = [ym, y2, y, yp]
     for k in range(1, up_steps + 1):
         w_step(k)
         if k == up_steps // 2:
@@ -200,13 +192,14 @@
         if k == up_steps - 1:
             pass_on(ym, 1)
             pass_on(yp, 0)
-    for k in range(3):
-        multiply(k, order[k])
+    multiply(0, order[0])
     pass_on(y2, 0)
     pass_on(y2, 1)
+    multiply(1, order[1])
+    multiply(2, order[2])
     combine(0, order[0])
     multiply(3, order[3])
-    for k in range(1, 4):
+    for k in range(1, NY):
         combine(k, order[k])
 
     seq = BLK * br
@@ -252,7 +245,7 @@
     smem = pl.BlockSpec(memory_space=pltpu.SMEM)
     hbm = pl.BlockSpec(memory_space=pl.ANY)
     chip_rows = NC * WORKB * br
-    parts = WCUT * WCUT
+    parts = W_ROW_CUT * W_COL_CUT
     head_grad, stats = pl.pallas_call(
         functools.partial(kernel, nz, nx),
         out_shape=(jax.ShapeDtypeStruct((seq, cols), bf16), jax.ShapeDtypeStruct((8, seq), jnp.float32)),

time: 92.9 us -> 87.7 us (0.944); the launches traced: 91.4 us -> 87.2 us
  Pallas kernels: 86.7 us -> 82.4 us
    pallas_call x1, Pallas kernels: 86.7 us -> 82.4 us  [shards(): pl.pallas_call(functools.partial(kernel, nz, nx), out_shape=(jax.ShapeDty...]
where the time goes in v3:
time: 87.7 us; the launch traced here: 87.2 us
  Pallas kernels  82.4 us (94%)
  other arithmetic  3.95 us (5%)
    pallas_call x1, Pallas kernels, shards(): pl.pallas_call(functools.partial(kernel, nz, nx), out_shape=(jax.ShapeDty...  82.4 us
    convert_element_type x1, other arithmetic, shards(): return result.astype(bf16)  3.14 us

profile of v3, /device:TPU:1, one launch (start us, length us, event | category | flops | bytes accessed | tf_op | source)
XLA Modules:
  0.0 87.2 jit_solution(17448206342934965034)
XLA Ops:
  0.0 0.0 copy-start.1
  0.0 0.0 copy-start
  0.7 82.4 %shard_map.82 = (bf16[512,1024]{1,0:T(8,128)(2,1)}, f32[8,512]{1,0:T(8,128)}) custom-call(s32[1,4]{1,0:T(1,128)} %slot_ref.1, s32[1]{0:T(128)S(6)} %copy.9.count_ref, s32[1,512]{1,0:T(1,128)} %bitcast.8, f32[1,1024]{1,0:T(1,128)} %bitcast.6, bf16[512,1024]{1,0:T(8,128)(2,1)} %hid_ref.1, bf16[256,1536]{1,0:T(8,128)(2,1)} %c_ref.1, bf16[32,1536]{1,0:T(8,128)(2,1)} %w_ref.1), custom_call_target="tpu_custom_call" | custom-call | tf_op jit(solution)/shard_map/pallas_call | solution.py:249
  83.2 0.8 add_rsqrt_fusion
  84.0 0.0 copy-done.1
  84.0 0.0 copy-done
  84.0 3.1 %subtract_convert_fusion = bf16[512,1024]{1,0:T(8,128)(2,1)} fusion(bf16[512,1024]{1,0:T(8,128)(2,1)S(1)} %copy-done, bf16[512,1024]{1,0:T(8,128)(2,1)} %get-tuple-element.8, bf16[512,1024]{1,0:T(8,128)(2,1)} %param.9, f32[512]{0:T(512)S(1)} %fusion.1, f32[1024]{0:T(1024)S(1)} %copy-done.1, f32[512]{0:T(512)S(1)} %bitcast.5), kind=kLoop, calls=%fused_computation | loop fusion | flops 4718592 | bytes 4202496 | tf_op jit(solution)/shard_map/convert_element_type | solution.py:288
  (1 shorter events, 0.0 us)
Async XLA Ops:
  0.0 84.0 %copy-start.1 = (f32[1024]{0:T(1024)S(1)}, f32[1024]{0:T(1024)}, u32[]{:S(2)}) copy-start(f32[1024]{0:T(1024)} %param.12) | copy-start | bytes 12292
  0.0 84.0 %copy-start = (bf16[512,1024]{1,0:T(8,128)(2,1)S(1)}, bf16[512,1024]{1,0:T(8,128)(2,1)}, u32[]{:S(2)}) copy-start(bf16[512,1024]{1,0:T(8,128)(2,1)} %hid_ref.1) | copy-start | bytes 3145732

commit v4 on v3

--- a/solution.py
+++ b/solution.py
@@ -14,6 +14,9 @@
 NY = 4
 NC = 2
 PLANE = NY * NC
+REACHED = (REACH + NC - 1 + NC - 1) // NC
+SLOTS = (REACH + NC - 1) * WORKB
+STAGES = (-1, 2, 0, 1)
 W_ROW_CUT = 2
 W_COL_CUT = 1
 MESH = pl.DeviceIdType.MESH
@@ -35,6 +38,7 @@
     shards = nz * PLANE
     yp, ym, y2 = lax.rem(y + 1, NY), lax.rem(y + 3, NY), lax.rem(y + 2, NY)
     plane = z * PLANE
+    xp, xl, x2 = lax.rem(x + 1, nx), lax.rem(x + nx - 1, nx), lax.rem(x + 2, nx)
     sibling = plane + y * NC + 1 - c
     above, below = plane + yp * NC + c, plane + ym * NC + c
     z_up, z_down = lax.rem(me + PLANE, shards), lax.rem(me + shards - PLANE, shards)
@@ -144,46 +148,75 @@
         for xx in range(nx):
             ps[xx, yy] = part[xx * pn:(xx + 1) * pn]
 
-        for r in range(1, nx):
-            xx = lax.rem(x + r, nx)
-            i = k * (nx - 1) + r - 1
-            go(remote(ps.at[xx, yy], xr.at[r - 1, yy], x_send.at[i], x_recv.at[i], me, xx))
+        send_x(k, yy, 0, 0, x2, xl)
+        send_x(k, yy, 0, 1, x2, xp)
+        send_x(k, yy, 1, 0, xp, xp)
+        send_x(k, yy, 1, 1, xl, xl)
+
+    def half_x(half):
+        return pl.ds(half * WORKB * br, WORKB * br)
+
+    def send_x(k, yy, kind, half, xx, to):
+        i = (k * 3 + kind) * NC + half
+        go(remote(
+            ps.at[xx, yy, :, half_x(half)], xr.at[kind, yy, :, half_x(half)], x_send.at[i], x_recv.at[i], me, to
+        ))
+
+    def wait_x(k, yy, kind, half):
+        landed(xr.at[kind, yy, :, half_x(half)], x_recv.at[(k * 3 + kind) * NC + half])
+
+    def relay(k, yy):
+        for half, to in ((0, xl), (1, xp)):
+            wait_x(k, yy, 0, half)
+            own = ps[to, yy, :, half_x(half)].astype(jnp.float32)
+            both = own + xr[0, yy, :, half_x(half)].astype(jnp.float32)
+            ps[to, yy, :, half_x(half)] = both.astype(jnp.bfloat16)
+            send_x(k, yy, 2, half, to, to)
 
     def combine(k, yy):
         total = ps[x, yy].astype(jnp.float32)
-        for r in range(1, nx):
-            landed(xr.at[r - 1, yy], x_recv.at[k * (nx - 1) + r - 1])
-            total = total + xr[r - 1, yy].astype(jnp.float32)
+        for kind in (1, 2):
+            for half in range(NC):
+                wait_x(k, yy, kind, half)
+            total = total + xr[kind, yy].astype(jnp.float32)
         total = total.astype(jnp.bfloat16)
         for s in range(NC * WORKB):
             sb[yy, s] = total[:, s * br:(s + 1) * br].reshape(sb.shape[2:])
-        for cc in range(NC):
-            for o in range(REACH):
-                dest = dest_of(yy, cc, o)
-
-                @pl.when(dest == me)
-                def _():
-                    pltpu.make_async_copy(*route(yy, cc, o)).start()
-
-                @pl.when(dest != me)
-                def _():
-                    deliver(k, yy, cc, o).start()
-
-    def dest_of(yy, cc, o):
-        return lax.rem(plane + yy * NC + cc - o + shards, shards)
-
-    def candidates(o, source):
-        return rb.at[pl.ds(o * WORKB, WORKB), :, source]
-
-    def route(yy, cc, o):
-        from_ref = sb.at[yy, pl.ds(cc * WORKB, WORKB)]
-        return from_ref, candidates(o, lane), s_recv.at[lane * REACH + o]
-
-    def deliver(k, yy, cc, o):
-        from_ref, to_ref, recv = route(yy, cc, o)
-        return remote(from_ref, to_ref, s_send.at[(k * NC + cc) * REACH + o], recv, dest_of(yy, cc, o), x)
-
-    order = [ym, y2, y, yp]
+        for d in range(REACHED):
+            dest = dest_of(yy, d)
+
+            @pl.when(dest == me)
+            def _():
+                pltpu.make_async_copy(*route(yy, d)).start()
+
+            @pl.when(dest != me)
+            def _():
+                deliver(k, yy, d).start()
+
+    def dest_of(yy, d):
+        chip = lax.rem(z * NY + yy - d + nz * NY, nz * NY)
+        return chip * NC + c
+
+    def union(d, source):
+        count = min(NC * WORKB, SLOTS - d * NC * WORKB)
+        return rb.at[pl.ds(d * NC * WORKB, count), :, source]
+
+    def route(yy, d):
+        to_ref = union(d, lane)
+        return sb.at[yy, pl.ds(0, to_ref.shape[0])], to_ref, s_recv.at[lane * REACHED + d]
+
+    def deliver(k, yy, d):
+        from_ref, to_ref, recv = route(yy, d)
+        return remote(from_ref, to_ref, s_send.at[k * REACHED + d], recv, dest_of(yy, d), x)
+
+    def share(k):
+        for d in range(REACHED):
+            source = lax.rem(y + d - STAGES[k] + NY, NY) * NC + c
+            at, recv = union(d, source), s_recv.at[source * REACHED + d]
+            landed(at, recv)
+            go(remote(at, at, s_send.at[(NY + k) * REACHED + d], recv, sibling, x))
+
+    order = [lax.rem(y + step + NY, NY) for step in STAGES]
     for k in range(1, up_steps + 1):
         w_step(k)
         if k == up_steps // 2:
@@ -196,21 +229,31 @@
     pass_on(y2, 0)
     pass_on(y2, 1)
     multiply(1, order[1])
+    relay(0, order[0])
     multiply(2, order[2])
+    relay(1, order[1])
     combine(0, order[0])
     multiply(3, order[3])
-    for k in range(1, NY):
-        combine(k, order[k])
+    relay(2, order[2])
+    combine(1, order[1])
+    share(0)
+    relay(3, order[3])
+    combine(2, order[2])
+    share(1)
+    combine(3, order[3])
+    share(2)
+    share(3)
 
     seq = BLK * br
     target = jnp.where(lax.broadcasted_iota(jnp.int32, (1, seq), 1) < count_ref[0], pos_ref[...], seq)
     place = (lax.broadcasted_iota(jnp.int32, (seq, seq), 0) == target).astype(jnp.float32).astype(jnp.bfloat16)
-    for s in range(PLANE):
-        for o in range(REACH):
-            landed(candidates(o, s), s_recv.at[s * REACH + o])
+    for yy in range(NY):
+        for d in range(REACHED):
+            source = yy * NC + 1 - c
+            landed(union(d, source), s_recv.at[source * REACHED + d])
     for b in range(BLK):
         v = slot_ref[0, b]
-        block = rb[jnp.maximum(v, 0)].reshape(rt.shape[0], br)
+        block = rb[jnp.maximum(v, 0) + WORKB * c].reshape(rt.shape[0], br)
         rt[:, b * br:(b + 1) * br] = jnp.where(v >= 0, block, jnp.zeros_like(block))
     placed = lax.dot_general(place, rt[...], NT, preferred_element_type=jnp.float32)
     grad_ref[...] = placed.astype(jnp.bfloat16)
@@ -226,11 +269,10 @@
     for copy in pending:
         copy.wait_send()
     for k in range(NY):
-        for cc in range(NC):
-            for o in range(REACH):
-                @pl.when(dest_of(order[k], cc, o) != me)
-                def _():
-                    deliver(k, order[k], cc, o).wait_send()
+        for d in range(REACHED):
+            @pl.when(dest_of(order[k], d) != me)
+            def _():
+                deliver(k, order[k], d).wait_send()
 
 
 def shards(nz, nx, hidden_in, grad_out, grad_qkv, qkv_weight, norm_gain, image_count, image_pos, block_slot):
@@ -255,9 +297,9 @@
             pltpu.VMEM((NY, chip_rows, depth), bf16),
             pltpu.VMEM((nz * wr, depth), bf16),
             pltpu.VMEM((nx, NY, pn, chip_rows), bf16),
-            pltpu.VMEM((nx - 1, NY, pn, chip_rows), bf16),
+            pltpu.VMEM((3, NY, pn, chip_rows), bf16),
             pltpu.VMEM((NY, NC * WORKB, nz // nx, wr, br), bf16),
-            pltpu.VMEM((REACH * WORKB, nz // nx, PLANE, wr, br), bf16),
+            pltpu.VMEM((SLOTS, nz // nx, PLANE, wr, br), bf16),
             pltpu.VMEM((cols, seq), bf16),
             pltpu.VMEM((seq, cols), bf16),
             pltpu.VMEM((nx, 8, seq), jnp.float32),
@@ -265,10 +307,10 @@
             dma((PLANE * WORKB,)),
             dma((2 * nz * parts,)),
             dma((nz * parts,)),
-            dma((NY * (nx - 1),)),
-            dma((NY * (nx - 1),)),
-            dma((PLANE * REACH,)),
-            dma((PLANE * REACH,)),
+            dma((NY * 3 * NC,)),
+            dma((NY * 3 * NC,)),
+            dma((2 * NY * REACHED,)),
+            dma((PLANE * REACHED,)),
             dma((nx - 1,)),
             dma((nx - 1,)),
             dma((3,)),

time: 87.7 us -> 84.4 us (0.962)
  Pallas kernels: 82.4 us -> 79.3 us
    pallas_call x1, Pallas kernels: 82.4 us -> 79.3 us  [shards(): pl.pallas_call(functools.partial(kernel, nz, nx), out_shape=(jax.ShapeDty...]
where the time goes in v4:
time: 84.4 us; the launch traced here: 84.1 us
  Pallas kernels  79.3 us (94%)
  other arithmetic  3.95 us (5%)
    pallas_call x1, Pallas kernels, shards(): pl.pallas_call(functools.partial(kernel, nz, nx), out_shape=(jax.ShapeDty...  79.3 us
    convert_element_type x1, other arithmetic, shards(): return result.astype(bf16)  3.14 us

profile of v4, /device:TPU:1, one launch (start us, length us, event | category | flops | bytes accessed | tf_op | source)
XLA Modules:
  0.0 84.1 jit_solution(5353267673502521549)
XLA Ops:
  0.0 0.0 copy-start.1
  0.0 0.0 copy-start
  0.7 79.3 %shard_map.82 = (bf16[512,1024]{1,0:T(8,128)(2,1)}, f32[8,512]{1,0:T(8,128)}) custom-call(s32[1,4]{1,0:T(1,128)} %slot_ref.1, s32[1]{0:T(128)S(6)} %copy.9.count_ref, s32[1,512]{1,0:T(1,128)} %bitcast.8, f32[1,1024]{1,0:T(1,128)} %bitcast.6, bf16[512,1024]{1,0:T(8,128)(2,1)} %hid_ref.1, bf16[256,1536]{1,0:T(8,128)(2,1)} %c_ref.1, bf16[32,1536]{1,0:T(8,128)(2,1)} %w_ref.1), custom_call_target="tpu_custom_call" | custom-call | tf_op jit(solution)/shard_map/pallas_call | solution.py:291
  80.1 0.8 add_rsqrt_fusion
  80.9 0.0 copy-done.1
  80.9 0.0 copy-done
  80.9 3.1 %subtract_convert_fusion = bf16[512,1024]{1,0:T(8,128)(2,1)} fusion(bf16[512,1024]{1,0:T(8,128)(2,1)S(1)} %copy-done, bf16[512,1024]{1,0:T(8,128)(2,1)} %get-tuple-element.8, bf16[512,1024]{1,0:T(8,128)(2,1)} %param.9, f32[512]{0:T(512)S(1)} %fusion.1, f32[1024]{0:T(1024)S(1)} %copy-done.1, f32[512]{0:T(512)S(1)} %bitcast.5), kind=kLoop, calls=%fused_computation | loop fusion | flops 4718592 | bytes 4202496 | tf_op jit(solution)/shard_map/convert_element_type | solution.py:330
  (1 shorter events, 0.0 us)
Async XLA Ops:
  0.0 80.9 %copy-start.1 = (f32[1024]{0:T(1024)S(1)}, f32[1024]{0:T(1024)}, u32[]{:S(2)}) copy-start(f32[1024]{0:T(1024)} %param.12) | copy-start | bytes 12292
  0.0 80.9 %copy-start = (bf16[512,1024]{1,0:T(8,128)(2,1)S(1)}, bf16[512,1024]{1,0:T(8,128)(2,1)}, u32[]{:S(2)}) copy-start(bf16[512,1024]{1,0:T(8,128)(2,1)} %hid_ref.1) | copy-start | bytes 3145732

commit v5 on v4

--- a/solution.py
+++ b/solution.py
@@ -24,8 +24,8 @@
 
 
 def kernel(
-    nz, nx, slot_ref, count_ref, pos_ref, gain_ref, hid_ref, c_ref, w_ref, grad_ref, stat_ref,
-    cg, wg, ps, xr, sb, rb, rt, hid, stats,
+    nz, nx, slot_ref, count_ref, pos_ref, gain_ref, hid_ref, go_ref, c_ref, w_ref, out_ref,
+    cg, wg, ps, xr, sb, rb, rt, hid, gout, stats,
     c_send, c_recv, w_send, w_recv, x_send, x_recv, s_send, s_recv, t_send, t_recv, own_sem,
 ):
     br = c_ref.shape[0] // WORKB
@@ -75,6 +75,8 @@
     own_c.start()
     own_w.start()
     own_h.start()
+    own_g = pltpu.make_async_copy(go_ref, gout, own_sem.at[3])
+    own_g.start()
     pl.semaphore_wait(barrier, 2 + (PLANE - 1) + (nx - 1))
 
     pending = []
@@ -219,7 +221,7 @@
     order = [lax.rem(y + step + NY, NY) for step in STAGES]
     for k in range(1, up_steps + 1):
         w_step(k)
-        if k == up_steps // 2:
+        if k == 3:
             pass_on(ym, 0, above)
             pass_on(yp, 1, below)
         if k == up_steps - 1:
@@ -256,15 +258,23 @@
         block = rb[jnp.maximum(v, 0) + WORKB * c].reshape(rt.shape[0], br)
         rt[:, b * br:(b + 1) * br] = jnp.where(v >= 0, block, jnp.zeros_like(block))
     placed = lax.dot_general(place, rt[...], NT, preferred_element_type=jnp.float32)
-    grad_ref[...] = placed.astype(jnp.bfloat16)
-    stats[0, 1:2, :] = row_sums(placed * gain_ref[...] * hid[...].astype(jnp.float32))
+    scaled = placed * gain_ref[...]
+    stats[0, 1:2, :] = row_sums(scaled * hid[...].astype(jnp.float32))
     for r in range(1, nx):
         go(remote(stats.at[0], stats.at[r], t_send.at[r - 1], t_recv.at[r - 1], me, lax.rem(x + r, nx)))
     total = stats[0]
     for r in range(1, nx):
         landed(stats.at[r], t_recv.at[r - 1])
         total = total + stats[r]
-    stat_ref[...] = total
+    own_g.wait()
+    inv_rms = lax.rsqrt(total[0:1] / D + 1e-05)
+    pull = inv_rms * inv_rms * inv_rms * total[1:2] / D
+    inv_rms = jnp.broadcast_to(inv_rms, (128, seq)).T
+    pull = jnp.broadcast_to(pull, (128, seq)).T
+    for t in range(out_ref.shape[1] // 128):
+        at = slice(t * 128, (t + 1) * 128)
+        grown = gout[:, at].astype(jnp.float32) + inv_rms * scaled[:, at]
+        out_ref[:, at] = (grown - hid[:, at].astype(jnp.float32) * pull).astype(jnp.bfloat16)
 
     for copy in pending:
         copy.wait_send()
@@ -288,11 +298,11 @@
     hbm = pl.BlockSpec(memory_space=pl.ANY)
     chip_rows = NC * WORKB * br
     parts = W_ROW_CUT * W_COL_CUT
-    head_grad, stats = pl.pallas_call(
+    return pl.pallas_call(
         functools.partial(kernel, nz, nx),
-        out_shape=(jax.ShapeDtypeStruct((seq, cols), bf16), jax.ShapeDtypeStruct((8, seq), jnp.float32)),
-        in_specs=[smem, smem, vmem, vmem, hbm, hbm, hbm],
-        out_specs=(vmem, vmem),
+        out_shape=jax.ShapeDtypeStruct((seq, cols), bf16),
+        in_specs=[smem, smem, vmem, vmem, hbm, hbm, hbm, hbm],
+        out_specs=vmem,
         scratch_shapes=[
             pltpu.VMEM((NY, chip_rows, depth), bf16),
             pltpu.VMEM((nz * wr, depth), bf16),
@@ -301,6 +311,7 @@
             pltpu.VMEM((NY, NC * WORKB, nz // nx, wr, br), bf16),
             pltpu.VMEM((SLOTS, nz // nx, PLANE, wr, br), bf16),
             pltpu.VMEM((cols, seq), bf16),
+            pltpu.VMEM((seq, cols), bf16),
             pltpu.VMEM((seq, cols), bf16),
             pltpu.VMEM((nx, 8, seq), jnp.float32),
             dma((14,)),
@@ -313,21 +324,12 @@
             dma((PLANE * REACHED,)),
             dma((nx - 1,)),
             dma((nx - 1,)),
-            dma((3,)),
+            dma((4,)),
         ],
         compiler_params=pltpu.CompilerParams(
             collective_id=0, has_side_effects=True, vmem_limit_bytes=60 * 1024 * 1024
         ),
-    )(block_slot, image_count, image_pos[None, :], norm_gain[None, :], hidden_in, grad_qkv, qkv_weight)
-
-    squares, cross = stats[0], stats[1]
-    inv_rms = lax.rsqrt(squares / D + 1e-05)
-    result = (
-        grad_out.astype(jnp.float32)
-        + inv_rms[:, None] * (head_grad.astype(jnp.float32) * norm_gain[None, :])
-        - hidden_in.astype(jnp.float32) * (inv_rms**3 * cross / D)[:, None]
-    )
-    return result.astype(bf16)
+    )(block_slot, image_count, image_pos[None, :], norm_gain[None, :], hidden_in, grad_out, grad_qkv, qkv_weight)
 
 
 def solution(mesh):

time: 84.4 us -> 82.9 us (0.982)
  other arithmetic: 3.95 us -> 0 us
  local copies, waits for them, and re-layouts: 0.01 us -> 2.26 us
    convert_element_type x1 -> x0, other arithmetic: 3.14 us -> none  [shards(): return result.astype(bf16)]
    unnamed x4 -> x1, local copies, waits for them, and re-layouts: 0.01 us -> 2.26 us
where the time goes in v5:
time: 82.9 us; the launch traced here: 82.7 us
  Pallas kernels  79.8 us (96%)
  local copies, waits for them, and re-layouts  2.26 us (3%)
    pallas_call x1, Pallas kernels, shards(): pl.pallas_call(functools.partial(kernel, nz, nx), out_shape=jax.ShapeDtyp...  79.8 us
    unnamed x1, local copies, waits for them, and re-layouts  2.26 us

profile of v5, /device:TPU:1, one launch (start us, length us, event | category | flops | bytes accessed | tf_op | source)
XLA Modules:
  0.0 82.7 jit_solution(429537075063901905)
XLA Ops:
  0.7 79.8 %shard_map.82 = bf16[512,1024]{1,0:T(8,128)(2,1)} custom-call(s32[1,4]{1,0:T(1,128)} %slot_ref.1, s32[1]{0:T(128)S(6)} %copy.10.count_ref, s32[1,512]{1,0:T(1,128)} %bitcast.3, f32[1,1024]{1,0:T(1,128)} %bitcast.2, bf16[512,1024]{1,0:T(8,128)(2,1)} %hid_ref.1, bf16[512,1024]{1,0:T(8,128)(2,1)} %go_ref.1, bf16[256,1536]{1,0:T(8,128)(2,1)} %c_ref.1, ...), custom_call_target="tpu_custom_call" | custom-call | tf_op jit(solution)/shard_map/pallas_call | solution.py:301
  80.5 2.3 %copy.11 = bf16[512,1024]{1,0:T(8,128)(2,1)} copy(bf16[512,1024]{1,0:T(8,128)(2,1)} %shard_map.82) | data formatting | bytes 2097152

commit v6 on v5

--- a/solution.py
+++ b/solution.py
@@ -85,6 +85,11 @@
         copy.start()
         pending.append(copy)
 
+    def drain(count):
+        for copy in pending[:count]:
+            copy.wait_send()
+        del pending[:count]
+
     def slot_at(yy, cc, h):
         return cg.at[yy, pl.ds(pl.multiple_of((cc * WORKB + h) * br, 16), br)]
 
@@ -227,6 +232,7 @@
         if k == up_steps - 1:
             pass_on(ym, 1)
             pass_on(yp, 0)
+    gathers = len(pending)
     multiply(0, order[0])
     pass_on(y2, 0)
     pass_on(y2, 1)
@@ -238,6 +244,7 @@
     multiply(3, order[3])
     relay(2, order[2])
     combine(1, order[1])
+    drain(gathers)
     share(0)
     relay(3, order[3])
     combine(2, order[2])
@@ -247,7 +254,7 @@
     share(3)
 
     seq = BLK * br
-    target = jnp.where(lax.broadcasted_iota(jnp.int32, (1, seq), 1) < count_ref[0], pos_ref[...], seq)
+    target = jnp.where(lax.broadcasted_iota(jnp.int32, (1, seq), 1) < count_ref[...], pos_ref[...], seq)
     place = (lax.broadcasted_iota(jnp.int32, (seq, seq), 0) == target).astype(jnp.float32).astype(jnp.bfloat16)
     for yy in range(NY):
         for d in range(REACHED):
@@ -262,6 +269,12 @@
     stats[0, 1:2, :] = row_sums(scaled * hid[...].astype(jnp.float32))
     for r in range(1, nx):
         go(remote(stats.at[0], stats.at[r], t_send.at[r - 1], t_recv.at[r - 1], me, lax.rem(x + r, nx)))
+    drain(len(pending) - 3)
+    for k in range(NY):
+        for d in range(REACHED):
+            @pl.when(dest_of(order[k], d) != me)
+            def _():
+                deliver(k, order[k], d).wait_send()
     total = stats[0]
     for r in range(1, nx):
         landed(stats.at[r], t_recv.at[r - 1])
@@ -275,14 +288,7 @@
         at = slice(t * 128, (t + 1) * 128)
         grown = gout[:, at].astype(jnp.float32) + inv_rms * scaled[:, at]
         out_ref[:, at] = (grown - hid[:, at].astype(jnp.float32) * pull).astype(jnp.bfloat16)
-
-    for copy in pending:
-        copy.wait_send()
-    for k in range(NY):
-        for d in range(REACHED):
-            @pl.when(dest_of(order[k], d) != me)
-            def _():
-                deliver(k, order[k], d).wait_send()
+    drain(3)
 
 
 def shards(nz, nx, hidden_in, grad_out, grad_qkv, qkv_weight, norm_gain, image_count, image_pos, block_slot):
@@ -301,7 +307,7 @@
     return pl.pallas_call(
         functools.partial(kernel, nz, nx),
         out_shape=jax.ShapeDtypeStruct((seq, cols), bf16),
-        in_specs=[smem, smem, vmem, vmem, hbm, hbm, hbm, hbm],
+        in_specs=[smem, vmem, vmem, vmem, hbm, hbm, hbm, hbm],
         out_specs=vmem,
         scratch_shapes=[
             pltpu.VMEM((NY, chip_rows, depth), bf16),
@@ -329,7 +335,7 @@
         compiler_params=pltpu.CompilerParams(
             collective_id=0, has_side_effects=True, vmem_limit_bytes=60 * 1024 * 1024
         ),
-    )(block_slot, image_count, image_pos[None, :], norm_gain[None, :], hidden_in, grad_out, grad_qkv, qkv_weight)
+    )(block_slot, image_count[None, :], image_pos[None, :], norm_gain[None, :], hidden_in, grad_out, grad_qkv, qkv_weight)
 
 
 def solution(mesh):

time: 82.9 us -> 82.8 us (level)
  no operation moved by 1% of the time
where the time goes in v6:
time: 82.8 us; the launch traced here: 82.6 us
  Pallas kernels  79.7 us (96%)
  local copies, waits for them, and re-layouts  2.26 us (3%)
    pallas_call x1, Pallas kernels, shards(): pl.pallas_call(functools.partial(kernel, nz, nx), out_shape=jax.ShapeDtyp...  79.7 us
    unnamed x1, local copies, waits for them, and re-layouts  2.26 us

profile of v6, /device:TPU:1, one launch (start us, length us, event | category | flops | bytes accessed | tf_op | source)
XLA Modules:
  0.0 82.6 jit_solution(10399997992348046598)
XLA Ops:
  0.7 79.7 %shard_map.82 = bf16[512,1024]{1,0:T(8,128)(2,1)} custom-call(s32[1,4]{1,0:T(1,128)} %slot_ref.1, s32[1,1]{1,0:T(1,128)} %bitcast.3.count_ref, s32[1,512]{1,0:T(1,128)} %bitcast.5, f32[1,1024]{1,0:T(1,128)} %bitcast.4, bf16[512,1024]{1,0:T(8,128)(2,1)} %hid_ref.1, bf16[512,1024]{1,0:T(8,128)(2,1)} %go_ref.1, bf16[256,1536]{1,0:T(8,128)(2,1)} %c_ref.1, ...), custom_call_target="tpu_custom_call" | custom-call | tf_op jit(solution)/shard_map/pallas_call | solution.py:307
  80.3 2.3 %copy.11 = bf16[512,1024]{1,0:T(8,128)(2,1)} copy(bf16[512,1024]{1,0:T(8,128)(2,1)} %shard_map.82) | data formatting | bytes 2097152
